TPU v7x, 512 devices: a whole 4x8x8 slice. The times are simulated.
512 devices in a mesh: ia: 16 (over z_lo, x, core), ja: 8 (over y), ka: 4 (over z_hi).
Axes of the slice: x: 4, y: 8, z: 8 (z_hi: 4, z_lo: 2; z = z_hi * 2 + z_lo), core: 2. Of those that a mesh axis runs over, the one named last changes fastest.
Arguments:
- tensor: float32 [512, 1024, 512], P('ia', 'ja', 'ka'), may hold values from -200 to 200
- factor_b: float32 [1024, 4, 96], P(('ja', 'ka')), may hold values from -4 to 4
- factor_c: float32 [512, 4, 96], P(('ka', 'ja')), may hold values from -4 to 4
Outputs:
- factor_a: float32 [512, 4, 96], P(('ia', 'ja', 'ka'))
- weights: float32 [4, 96], replicated
All inputs are finite; a program needn't handle non-finite values.
Results may differ from a plain program's by a relative error of at most 0.0003.
Values sent between devices are 32-bit elements; how exact they have to be, the bound alone decides.
No kernel may reach another device: no remote copies, remote signals or barrier semaphores. Data moves between devices by JAX's collectives and lax.ppermute only.
A program may use at most 64 MiB of HBM per device.

v0:
```python
import jax
import jax.numpy as jnp
from jax import lax
from jax.sharding import PartitionSpec as P

highest = lax.Precision.HIGHEST


def gram_of(rows):
    return jnp.einsum(
        "jsr,jsq->srq", rows, rows, precision=highest, preferred_element_type=jnp.float32
    )


def solve_normal(rows, gram_b, gram_c):
    columns = []
    for member in range(rows.shape[1]):
        normal_mat = gram_b[member] * gram_c[member]
        factor_l = jnp.linalg.cholesky(normal_mat)
        right_side = rows[:, member, :].T
        lower_sol = lax.linalg.triangular_solve(factor_l, right_side, left_side=True, lower=True)
        upper_sol = lax.linalg.triangular_solve(
            factor_l, lower_sol, left_side=True, lower=True, transpose_a=True
        )
        columns.append(upper_sol.T)
    return jnp.stack(columns, axis=1)


def shards(tensor, factor_b, factor_c):
    rows_i, rows_j, rows_k = tensor.shape
    starts, col_count = (factor_b.shape[1], factor_b.shape[2])
    width = starts * col_count
    c_block = lax.all_gather(factor_c, "ja", axis=0, tiled=True)
    partial_value = jnp.dot(
        tensor.reshape(rows_i * rows_j, rows_k),
        c_block.reshape(rows_k, width),
        precision=highest,
        preferred_element_type=jnp.float32,
    ).reshape(rows_i, rows_j, width)
    piece = lax.all_gather(factor_b, "ka", axis=0, tiled=True)
    gram_sum = jnp.zeros((starts, col_count, col_count), jnp.float32)
    count = piece.shape[0]
    flat_rows = piece.reshape(count, width)
    mttkrp = jnp.einsum(
        "ijr,jr->ir",
        partial_value,
        flat_rows,
        precision=highest,
        preferred_element_type=jnp.float32,
    )
    mttkrp, gram_rows = (mttkrp, gram_sum)
    gram_b, gram_c = lax.psum((gram_of(factor_b), gram_of(factor_c)), ("ja", "ka"))
    slab_rows = lax.psum_scatter(mttkrp, "ja", scatter_dimension=0, tiled=True)
    owned = lax.psum_scatter(slab_rows, "ka", scatter_dimension=0, tiled=True)
    owned = owned.reshape(owned.shape[0], starts, col_count)
    factor_raw = solve_normal(owned, gram_b, gram_c)
    squares = jnp.sum(factor_raw * factor_raw, axis=0)
    total = lax.psum(squares, ("ia", "ja", "ka"))
    row_total = rows_i * lax.axis_size("ia")
    weights = jnp.sqrt(total / row_total + 1e-06)
    return (factor_raw / weights[None], weights)


def solution(mesh):
    in_specs = (P("ia", "ja", "ka"), P(("ja", "ka"), None, None), P(("ka", "ja"), None, None))
    out_specs = (P(("ia", "ja", "ka"), None, None), P())
    return jax.shard_map(shards, mesh=mesh, in_specs=in_specs, out_specs=out_specs, check_vma=False)
```

profile of v0, /device:TPU:1, one launch (start us, length us, event | category | flops | bytes accessed | tf_op | source)
XLA Modules:
  0.0 503.4 jit_solution(228719153162087754)
XLA Ops:
  7.2 0.0 copy-start
  7.2 0.0 all-reduce.5.cloned.1.call-start
  7.2 2.1 fusion.22
  9.3 2.1 fusion
  11.4 0.0 all-reduce.5.cloned.1.call-update
  11.4 18.7 %all_gather.7 = f32[128,4,96]{2,1,0:T(4,128)S(1)} all-gather(f32[32,4,96]{2,1,0:T(4,128)} %param.9), channel_id=1, replica_groups=mesh['ia'=16,'ja'=8,'ka'=4] {'ka'}, dimensions={0}, use_global_device_ids=true | all-gather | bytes 245760 | tf_op jit(solution)/shard_map/all_gather | solution.py:40
  30.1 22.2 %all_gather.6 = f32[128,4,96]{2,1,0:T(4,128)S(1)} all-gather(f32[16,4,96]{2,1,0:T(4,128)} %param.10), channel_id=1, replica_groups=mesh['ia'=16,'ja'=8,'ka'=4] {'ja'}, dimensions={0}, use_global_device_ids=true | all-gather | bytes 221184 | tf_op jit(solution)/shard_map/all_gather | solution.py:33
  52.3 0.1 copy.51
  52.4 0.1 copy.52
  52.6 0.1 copy.34
  52.7 1.3 dynamic-slice
  54.0 1.3 dynamic-slice.2
  55.9 0.0 copy-done
  55.9 5.5 %multiply_reduce_fusion = f32[384,32]{0,1:T(8,128)S(1)} fusion(f32[384,128]{0,1:T(8,128)S(1)} %copy.52, f32[32,128,128]{2,1,0:T(8,128)S(1)} %copy-done, f32[128,384,1]{0,1,2:T(8,128)S(1)} %bitcast.141), kind=kOutput, calls=%fused_computation | convolution fusion | flops 2419052544 | bytes 2539520 | tf_op jit(solution)/shard_map/dot_general | solution.py:34
  61.4 23.5 %all-reduce = f32[32,384]{1,0:T(8,128)S(1)} all-reduce(f32[32,384]{1,0:T(8,128)S(1)} %bitcast.142), channel_id=2, replica_groups=mesh['ia'=16,'ja'=8,'ka'=4] {'ja'}, use_global_device_ids=true, to_apply=%region_4.0.clone | all-reduce | flops 12288 | bytes 98304
  84.9 9.5 %all-reduce.1 = f32[4,384]{1,0:T(4,128)S(1)} all-reduce(f32[4,384]{1,0:T(4,128)S(1)} %constant_dynamic-slice_fusion), channel_id=3, replica_groups=mesh['ia'=16,'ja'=8,'ka'=4] {'ka'}, use_global_device_ids=true, to_apply=%region_5.0.clone | all-reduce | flops 1536 | bytes 12288
  94.5 0.7 dynamic-slice_reduce_fusion
  95.1 0.1 reshape.87
  95.2 210.4 %all-reduce.5.cloned.1.call-done = (f32[4,96,96]{1,2,0:T(8,128)}, f32[4,96,96]{1,2,0:T(8,128)}) async-done(((f32[4,96,96]{1,2,0:T(8,128)}, f32[4,96,96]{1,2,0:T(8,128)}), (f32[4,96,96]{1,2,0:T(8,128)}, f32[4,96,96]{1,2,0:T(8,128)})) %all-reduce.5.cloned.1.call-update) | async-done | bytes 294928 | tf_op jit(solution)/shard_map/psum | solution.py:52
  305.6 1.0 fusion.24
  306.6 0.1 copy.33
  306.7 0.1 copy.39
  306.8 0.1 copy.38
  306.9 0.1 copy.37
  307.0 1.0 fusion.9
  308.0 8.8 %cholesky.107 = f32[96,96]{1,0:T(8,128)S(1)} custom-call(f32[96,96]{1,0:T(8,128)S(1)} %get-tuple-element.10), custom_call_target="Cholesky" | custom-call | tf_op jit(solution)/shard_map/jit(cholesky)/cholesky | solution.py:19
  316.8 0.6 compare_reduce_fusion
  317.5 0.7 fusion.5
  318.1 7.4 %custom-call.21 = f32[1,96,96]{1,2,0:T(8,128)S(1)} custom-call(f32[1,96,96]{2,1,0:T(8,128)S(1)} %fusion.5), custom_call_target="InvertDiagBlocksLowerTriangular" | custom-call | tf_op jit(solution)/shard_map/triangular_solve/custom-call.2 | solution.py:22
  325.5 0.1 convolution_bitcast_fusion
  325.6 0.2 fusion.11
  325.8 8.8 %cholesky.96 = f32[96,96]{1,0:T(8,128)S(1)} custom-call(f32[96,96]{1,0:T(8,128)S(1)} %get-tuple-element.11), custom_call_target="Cholesky" | custom-call | tf_op jit(solution)/shard_map/jit(cholesky)/cholesky | solution.py:19
  334.7 0.6 compare_reduce_fusion.1
  335.3 0.7 fusion.4
  336.0 7.4 %custom-call.19 = f32[1,96,96]{1,2,0:T(8,128)S(1)} custom-call(f32[1,96,96]{2,1,0:T(8,128)S(1)} %fusion.4), custom_call_target="InvertDiagBlocksLowerTriangular" | custom-call | tf_op jit(solution)/shard_map/triangular_solve/custom-call.2 | solution.py:22
  343.3 0.1 convolution_bitcast_fusion.1
  343.5 0.2 fusion.14
  343.7 8.8 %cholesky.85 = f32[96,96]{1,0:T(8,128)S(1)} custom-call(f32[96,96]{1,0:T(8,128)S(1)} %get-tuple-element.12), custom_call_target="Cholesky" | custom-call | tf_op jit(solution)/shard_map/jit(cholesky)/cholesky | solution.py:19
  352.5 0.6 compare_reduce_fusion.2
  353.1 0.7 fusion.3
  353.8 7.4 %custom-call.17 = f32[1,96,96]{1,2,0:T(8,128)S(1)} custom-call(f32[1,96,96]{2,1,0:T(8,128)S(1)} %fusion.3), custom_call_target="InvertDiagBlocksLowerTriangular" | custom-call | tf_op jit(solution)/shard_map/triangular_solve/custom-call.2 | solution.py:22
  361.2 0.1 convolution_bitcast_fusion.2
  361.3 0.2 fusion.17
  361.5 9.0 %cholesky.74 = f32[96,96]{1,0:T(8,128)S(1)} custom-call(f32[96,96]{1,0:T(8,128)S(1)} %get-tuple-element.9), custom_call_target="Cholesky" | custom-call | tf_op jit(solution)/shard_map/jit(cholesky)/cholesky | solution.py:19
  370.6 0.6 compare_reduce_fusion.3
  371.2 0.7 fusion.2
  371.9 7.4 %custom-call.15 = f32[1,96,96]{1,2,0:T(8,128)S(1)} custom-call(f32[1,96,96]{2,1,0:T(8,128)S(1)} %fusion.2), custom_call_target="InvertDiagBlocksLowerTriangular" | custom-call | tf_op jit(solution)/shard_map/triangular_solve/custom-call.2 | solution.py:22
  379.2 0.1 convolution_bitcast_fusion.3
  379.4 0.2 fusion.20
  379.6 116.4 %psum.23 = f32[4,96]{1,0:T(4,128)S(1)} all-reduce(f32[4,96]{1,0:T(4,128)S(1)} %fusion.36), channel_id=1, replica_groups=mesh['ia'=16,'ja'=8,'ka'=4] {'ia','ja','ka'}, use_global_device_ids=true, to_apply=%region_6.10 | all-reduce | flops 384 | bytes 3072 | tf_op jit(solution)/shard_map/psum | solution.py:58
  496.0 0.6 divide_bitcast_fusion
  (6 shorter events, 0.2 us)
Async XLA Ops:
  7.2 48.7 %copy-start = (f32[32,128,128]{2,1,0:T(8,128)S(1)}, f32[32,128,128]{2,1,0:T(8,128)}, u32[]{:S(2)}) copy-start(f32[32,128,128]{2,1,0:T(8,128)} %param.8) | copy-start | bytes 6291460
  7.2 298.5 %all-reduce.5.cloned.1.call-start = ((), (), s32[]{:S(2)}) async-start(), calls=%async_computation | async-start | bytes 786432 | tf_op jit(solution)/shard_map/psum | solution.py:52
Sparse Core Ops, SparseCore 0:
  11.5 294.0 all-reduce.4
where the time goes:
time: 504 us; the launch traced here: 503 us
  waiting for transfers between devices  210 us (42%)
  blocking collectives  190 us (38%)
  other arithmetic  72.8 us (14%)
  between operations  14.9 us (3%)
  matrix products  11 us (2%)
    psum x1, waiting for transfers between devices, shards(): lax.psum((gram_of(factor_b), gram_of(factor_c)), ('ja', 'ka'))  210 us
    psum x1, blocking collectives, shards(): total = lax.psum(squares, ('ia', 'ja', 'ka'))  116 us
    another operation x12, other arithmetic, solve_normal(): factor_l = jnp.linalg.cholesky(normal_mat)  38.1 us
    unnamed x2, blocking collectives  33 us
    another operation x8, other arithmetic, solve_normal(): lax.linalg.triangular_solve(factor_l, lower_sol, left_side=True, lower=Tr...  32 us
    all_gather x1, blocking collectives, shards(): c_block = lax.all_gather(factor_c, 'ja', axis=0, tiled=True)  22.2 us
    all_gather x1, blocking collectives, shards(): piece = lax.all_gather(factor_b, 'ka', axis=0, tiled=True)  18.7 us
  transfers between devices with their start and end apart: 1, of which 1 were waited for; matrix products, arithmetic and copies ran while one was open for 2% of the time, Pallas kernels for 0%

commit v1 on v0

--- a/solution.py
+++ b/solution.py
@@ -49,7 +49,7 @@
         preferred_element_type=jnp.float32,
     )
     mttkrp, gram_rows = (mttkrp, gram_sum)
-    gram_b, gram_c = lax.psum((gram_of(factor_b), gram_of(factor_c)), ("ja", "ka"))
+    gram_b, gram_c = lax.psum(lax.psum((gram_of(factor_b), gram_of(factor_c)), "ka"), "ja")
     slab_rows = lax.psum_scatter(mttkrp, "ja", scatter_dimension=0, tiled=True)
     owned = lax.psum_scatter(slab_rows, "ka", scatter_dimension=0, tiled=True)
     owned = owned.reshape(owned.shape[0], starts, col_count)

time: 504 us -> 334 us (0.66)
  waiting for transfers between devices: 210 us -> 55.6 us
  blocking collectives: 190 us -> 176 us
    psum x1 -> x2, waiting for transfers between devices: 210 us -> 55.6 us  [the longest x1 36.6 us: shards(): lax.psum(lax.psum((gram_of(factor_b), gram_of(factor_c)), 'ka'), 'ja')]
    psum x1, blocking collectives: 116 us -> 102 us  [shards(): total = lax.psum(squares, ('ia', 'ja', 'ka'))]
  transfers between devices with their start and end apart: 1 -> 2, of which waited for: 1 -> 2; matrix products, arithmetic and copies ran while one was open for 2% -> 3% of each run, Pallas kernels for 0% -> 0%
where the time goes in v1:
time: 334 us
  blocking collectives  176 us (53%)
  other arithmetic  72.8 us (22%)
  waiting for transfers between devices  55.6 us (17%)
  between operations  14.9 us (4%)
  matrix products  11 us (3%)
  local copies, waits for them, and re-layouts  4.02 us (1%)
    psum x1, blocking collectives, shards(): total = lax.psum(squares, ('ia', 'ja', 'ka'))  102 us
    another operation x12, other arithmetic, solve_normal(): factor_l = jnp.linalg.cholesky(normal_mat)  38.1 us
    psum x1, waiting for transfers between devices, shards(): lax.psum(lax.psum((gram_of(factor_b), gram_of(factor_c)), 'ka'), 'ja')  36.6 us
    unnamed x2, blocking collectives  33.1 us
    another operation x8, other arithmetic, solve_normal(): lax.linalg.triangular_solve(factor_l, lower_sol, left_side=True, lower=Tr...  32 us
    all_gather x1, blocking collectives, shards(): c_block = lax.all_gather(factor_c, 'ja', axis=0, tiled=True)  21.5 us
    psum x1, waiting for transfers between devices, shards(): lax.psum((gram_of(factor_b), gram_of(factor_c)), 'ka')  18.9 us
    all_gather x1, blocking collectives, shards(): piece = lax.all_gather(factor_b, 'ka', axis=0, tiled=True)  18.7 us
  transfers between devices with their start and end apart: 2, of which 2 were waited for; matrix products, arithmetic and copies ran while one was open for 3% of the time, Pallas kernels for 0%

profile of v1, /device:TPU:1, one launch (start us, length us, event | category | flops | bytes accessed | tf_op | source)
XLA Modules:
  0.0 334.0 jit_solution(149396167900332453)
XLA Ops:
  7.2 0.0 copy-start
  7.2 0.0 copy-start.1
  7.2 0.0 all-reduce.9.cloned.1.call-start
  7.2 2.1 fusion.22
  9.3 2.1 fusion
  11.4 0.0 all-reduce.9.cloned.1.call-update
  11.4 0.0 all-reduce.7.cloned.1.call-start
  11.5 18.7 %all_gather.7 = f32[128,4,96]{2,1,0:T(4,128)S(1)} all-gather(f32[32,4,96]{2,1,0:T(4,128)} %param.9), channel_id=1, replica_groups=mesh['ia'=16,'ja'=8,'ka'=4] {'ka'}, dimensions={0}, use_global_device_ids=true | all-gather | bytes 245760 | tf_op jit(solution)/shard_map/all_gather | solution.py:40
  30.2 0.1 copy.51
  30.3 0.1 copy.52
  30.5 0.0 copy-done.1
  30.5 21.5 %all_gather.6 = f32[128,4,96]{2,1,0:T(4,128)S(1)} all-gather(f32[16,4,96]{2,1,0:T(4,128)S(1)} %copy-done.1), channel_id=1, replica_groups=mesh['ia'=16,'ja'=8,'ka'=4] {'ja'}, dimensions={0}, use_global_device_ids=true | all-gather | bytes 221184 | tf_op jit(solution)/shard_map/all_gather | solution.py:33
  52.0 0.1 copy.34
  52.1 1.3 dynamic-slice
  53.4 1.3 dynamic-slice.2
  55.3 18.9 %all-reduce.9.cloned.1.call-done = (f32[4,96,96]{1,2,0:T(8,128)}, f32[4,96,96]{1,2,0:T(8,128)}) async-done(((f32[4,96,96]{1,2,0:T(8,128)}, f32[4,96,96]{1,2,0:T(8,128)}), (f32[4,96,96]{1,2,0:T(8,128)}, f32[4,96,96]{1,2,0:T(8,128)})) %all-reduce.9.cloned.1.call-update) | async-done | bytes 294928 | tf_op jit(solution)/shard_map/psum | solution.py:52
  74.2 0.0 all-reduce.7.cloned.1.call-update
  74.3 0.0 copy-done
  74.3 5.5 %multiply_reduce_fusion = f32[384,32]{0,1:T(8,128)S(1)} fusion(f32[384,128]{0,1:T(8,128)S(1)} %copy.52, f32[32,128,128]{2,1,0:T(8,128)S(1)} %copy-done, f32[128,384,1]{0,1,2:T(8,128)S(1)} %bitcast.141), kind=kOutput, calls=%fused_computation | convolution fusion | flops 2419052544 | bytes 2539520 | tf_op jit(solution)/shard_map/dot_general | solution.py:34
  79.8 23.5 %all-reduce = f32[32,384]{1,0:T(8,128)S(1)} all-reduce(f32[32,384]{1,0:T(8,128)S(1)} %bitcast.142), channel_id=2, replica_groups=mesh['ia'=16,'ja'=8,'ka'=4] {'ja'}, use_global_device_ids=true, to_apply=%region_6.0.clone | all-reduce | flops 12288 | bytes 98304
  103.3 9.6 %all-reduce.1 = f32[4,384]{1,0:T(4,128)S(1)} all-reduce(f32[4,384]{1,0:T(4,128)S(1)} %constant_dynamic-slice_fusion), channel_id=3, replica_groups=mesh['ia'=16,'ja'=8,'ka'=4] {'ka'}, use_global_device_ids=true, to_apply=%region_7.0.clone | all-reduce | flops 1536 | bytes 12288
  112.9 0.7 dynamic-slice_reduce_fusion
  113.6 0.1 reshape.87
  113.7 36.6 %all-reduce.7.cloned.1.call-done = (f32[4,96,96]{1,2,0:T(8,128)}, f32[4,96,96]{1,2,0:T(8,128)}) async-done(((f32[4,96,96]{1,2,0:T(8,128)}, f32[4,96,96]{1,2,0:T(8,128)}), (f32[4,96,96]{1,2,0:T(8,128)}, f32[4,96,96]{1,2,0:T(8,128)})) %all-reduce.7.cloned.1.call-update) | async-done | bytes 294928 | tf_op jit(solution)/shard_map/psum | solution.py:52
  150.3 1.0 fusion.24
  151.3 0.1 copy.33
  151.4 0.1 copy.39
  151.5 0.1 copy.38
  151.6 0.1 copy.37
  151.6 1.0 fusion.9
  152.7 8.8 %cholesky.107 = f32[96,96]{1,0:T(8,128)S(1)} custom-call(f32[96,96]{1,0:T(8,128)S(1)} %get-tuple-element.12), custom_call_target="Cholesky" | custom-call | tf_op jit(solution)/shard_map/jit(cholesky)/cholesky | solution.py:19
  161.5 0.6 compare_reduce_fusion
  162.1 0.7 fusion.5
  162.8 7.4 %custom-call.21 = f32[1,96,96]{1,2,0:T(8,128)S(1)} custom-call(f32[1,96,96]{2,1,0:T(8,128)S(1)} %fusion.5), custom_call_target="InvertDiagBlocksLowerTriangular" | custom-call | tf_op jit(solution)/shard_map/triangular_solve/custom-call.2 | solution.py:22
  170.1 0.1 convolution_bitcast_fusion
  170.3 0.2 fusion.11
  170.5 8.8 %cholesky.96 = f32[96,96]{1,0:T(8,128)S(1)} custom-call(f32[96,96]{1,0:T(8,128)S(1)} %get-tuple-element.13), custom_call_target="Cholesky" | custom-call | tf_op jit(solution)/shard_map/jit(cholesky)/cholesky | solution.py:19
  179.3 0.6 compare_reduce_fusion.1
  180.0 0.7 fusion.4
  180.6 7.4 %custom-call.19 = f32[1,96,96]{1,2,0:T(8,128)S(1)} custom-call(f32[1,96,96]{2,1,0:T(8,128)S(1)} %fusion.4), custom_call_target="InvertDiagBlocksLowerTriangular" | custom-call | tf_op jit(solution)/shard_map/triangular_solve/custom-call.2 | solution.py:22
  188.0 0.1 convolution_bitcast_fusion.1
  188.1 0.2 fusion.14
  188.3 8.8 %cholesky.85 = f32[96,96]{1,0:T(8,128)S(1)} custom-call(f32[96,96]{1,0:T(8,128)S(1)} %get-tuple-element.14), custom_call_target="Cholesky" | custom-call | tf_op jit(solution)/shard_map/jit(cholesky)/cholesky | solution.py:19
  197.2 0.6 compare_reduce_fusion.2
  197.8 0.7 fusion.3
  198.5 7.4 %custom-call.17 = f32[1,96,96]{1,2,0:T(8,128)S(1)} custom-call(f32[1,96,96]{2,1,0:T(8,128)S(1)} %fusion.3), custom_call_target="InvertDiagBlocksLowerTriangular" | custom-call | tf_op jit(solution)/shard_map/triangular_solve/custom-call.2 | solution.py:22
  205.8 0.1 convolution_bitcast_fusion.2
  206.0 0.2 fusion.17
  206.2 9.0 %cholesky.74 = f32[96,96]{1,0:T(8,128)S(1)} custom-call(f32[96,96]{1,0:T(8,128)S(1)} %get-tuple-element.11), custom_call_target="Cholesky" | custom-call | tf_op jit(solution)/shard_map/jit(cholesky)/cholesky | solution.py:19
  215.2 0.6 compare_reduce_fusion.3
  215.9 0.7 fusion.2
  216.5 7.4 %custom-call.15 = f32[1,96,96]{1,2,0:T(8,128)S(1)} custom-call(f32[1,96,96]{2,1,0:T(8,128)S(1)} %fusion.2), custom_call_target="InvertDiagBlocksLowerTriangular" | custom-call | tf_op jit(solution)/shard_map/triangular_solve/custom-call.2 | solution.py:22
  223.9 0.1 convolution_bitcast_fusion.3
  224.0 0.2 fusion.20
  224.3 102.3 %psum.39 = f32[4,96]{1,0:T(4,128)S(1)} all-reduce(f32[4,96]{1,0:T(4,128)S(1)} %fusion.36), channel_id=1, replica_groups=mesh['ia'=16,'ja'=8,'ka'=4] {'ia','ja','ka'}, use_global_device_ids=true, to_apply=%region_8.12 | all-reduce | flops 384 | bytes 3072 | tf_op jit(solution)/shard_map/psum | solution.py:58
  326.6 0.6 divide_bitcast_fusion
  (6 shorter events, 0.2 us)
Async XLA Ops:
  7.2 67.1 %copy-start = (f32[32,128,128]{2,1,0:T(8,128)S(1)}, f32[32,128,128]{2,1,0:T(8,128)}, u32[]{:S(2)}) copy-start(f32[32,128,128]{2,1,0:T(8,128)} %param.8) | copy-start | bytes 6291460
  7.2 23.3 %copy-start.1 = (f32[16,4,96]{2,1,0:T(4,128)S(1)}, f32[16,4,96]{2,1,0:T(4,128)}, u32[]{:S(2)}) copy-start(f32[16,4,96]{2,1,0:T(4,128)} %param.10) | copy-start | bytes 73732
  7.2 67.1 %all-reduce.9.cloned.1.call-start = ((), (), s32[]{:S(2)}) async-start(), calls=%async_computation.1 | async-start | bytes 786432 | tf_op jit(solution)/shard_map/psum | solution.py:52
  11.4 138.9 %all-reduce.7.cloned.1.call-start = ((), (), s32[]{:S(2)}) async-start(), calls=%async_computation | async-start | bytes 786432 | tf_op jit(solution)/shard_map/psum | solution.py:52
Sparse Core Ops, SparseCore 0:
  11.5 62.6 all-reduce.8
  76.7 73.5 all-reduce.6
